TPU v7x, 256 devices: a whole 4x4x8 slice. The times are simulated.
256 devices in a mesh: tm: 8 (over y, core), mp: 4 (over z_lo), tok: 8 (over z_hi, x).
Axes of the slice: x: 4, y: 4, z: 8 (z_hi: 2, z_lo: 4; z = z_hi * 4 + z_lo), core: 2. Of those that a mesh axis runs over, the one named last changes fastest.
Arguments:
- features: bfloat16 [1024, 3584], P('tok'), may hold values from -6 to 6
- spike_mask: int32 [8, 1024, 3584], P('tm', 'tok'), may hold values 0 or 1
- gate_weight: bfloat16 [3584, 7168], P(('tm', 'tok'), 'mp'), may hold values from -0.09375 to 0.09375
- threshold: float32 [7168], P('mp'), may hold values from 0.5 to 2
Outputs:
- rates: float32 [1024, 7168], P('tok', 'mp')
- grad_threshold: float32 [7168], P('mp')
All inputs are finite; a program needn't handle non-finite values. No bound on the sum of `spike_mask` on one device may be relied on, other than what follows from the above.
Results may differ from a plain program's by a relative error of at most 0.00035.
Values may be sent and summed in bfloat16 or wider, within the bound.
No kernel may reach another device: no remote copies, remote signals or barrier semaphores. Data moves between devices by JAX's collectives and lax.ppermute only.
A program may use at most 64 MiB of HBM per device.

v0:
```python
import jax
import jax.numpy as jnp
from jax import lax
from jax.sharding import PartitionSpec as P

SHARP = 2.0


def passed_along(x, axis, by):
    peers = lax.axis_size(axis)
    pairs = [(i, i + by) for i in range(peers) if 0 <= i + by < peers]
    return lax.ppermute(x, axis, pairs)


def on_device(features, spike_mask, gate_weight, threshold):
    steps = lax.axis_size("tm")
    step_index = lax.axis_index("tm")
    tokens_all = features.shape[0] * lax.axis_size("tok")
    rows = features.shape[0]
    width = gate_weight.shape[1]
    driven = jnp.where(spike_mask[0] > 0, features, jnp.zeros_like(features))
    piece = lax.all_gather(gate_weight, ("tm", "tok"), axis=0, tiled=True)
    student = jnp.dot(driven, piece, preferred_element_type=jnp.float32)
    teacher = jnp.dot(features, piece, preferred_element_type=jnp.float32)
    current = 2.0 * student
    target = jax.nn.silu(teacher)
    blocks = 1
    size = rows // blocks
    turns = steps + blocks - 1

    def forward_turn(turn, carry):
        incoming, spikes = carry
        block = turn - step_index
        active = (block >= 0) & (block < blocks)
        rising = incoming + current
        fired = jax.nn.sigmoid(SHARP * (rising - threshold))
        leaving = rising - threshold * fired
        older = spikes
        spikes = jnp.where(active, fired, older)
        passed = passed_along(leaving, "tm", 1)
        return (passed, spikes)

    block_zero = jnp.zeros((size, width), jnp.float32)
    unused, spikes = lax.fori_loop(
        0, turns, forward_turn, (block_zero, jnp.zeros((rows, width), jnp.float32))
    )
    total = lax.psum(spikes, "tm")
    rates = threshold * total / steps
    error = (rates - target) / tokens_all

    def backward_turn(turn, carry):
        incoming, grad_sum = carry
        block = turn - (steps - 1 - step_index)
        active = (block >= 0) & (block < blocks)
        dspike = error * threshold / steps - threshold * incoming
        dwide = dspike * SHARP * spikes * (1.0 - spikes)
        term = jnp.sum(-dwide - spikes * incoming + error * spikes / steps, axis=0)
        grad_sum = grad_sum + jnp.where(active, term, jnp.zeros_like(term))
        passed = passed_along((incoming + dwide).astype(jnp.bfloat16), "tm", -1).astype(jnp.float32)
        return (passed, grad_sum)

    unused_cot, grad_local = lax.fori_loop(
        0, turns, backward_turn, (block_zero, jnp.zeros((width,), jnp.float32))
    )
    grad_threshold = lax.psum(grad_local, ("tm", "tok"))
    return (rates, grad_threshold)


def solution(mesh):
    return jax.shard_map(
        on_device,
        mesh=mesh,
        in_specs=(P("tok", None), P("tm", "tok", None), P(("tm", "tok"), "mp"), P("mp")),
        out_specs=(P("tok", "mp"), P("mp")),
        check_vma=False,
    )
```

profile of v0, /device:TPU:32, one launch (start us, length us, event | category | flops | bytes accessed | tf_op | source)
XLA Modules:
  0.0 676.2 jit_solution(10581541776726929995)
XLA Ops:
  7.2 0.7 all-gather.2.cloned.1.call-update
  8.0 140.1 %all-gather.2.cloned.1.call-done = bf16[3584,1792]{1,0:T(8,128)(2,1)} async-done(((bf16[56,1792]{1,0:T(8,128)(2,1)}), bf16[3584,1792]{1,0:T(8,128)(2,1)}) %all-gather.2.cloned.1.call-update) | async-done | bytes 12845072 | tf_op jit(solution)/shard_map/all_gather | solution.py:22
  148.0 7.4 %convolution_multiply_fusion = f32[128,1792]{1,0:T(8,128)S(1)} fusion(bf16[3584,1792]{1,0:T(8,128)(2,1)} %all-gather.2.cloned.1.call-done, bf16[128,3584]{1,0:T(8,128)(2,1)} %param.8, s32[1,128,3584]{2,1,0:T(8,128)} %param.9), kind=kOutput, calls=%fused_computation.8 | convolution fusion | flops 1645314048 | bytes 16515072 | tf_op jit(solution)/shard_map/dot_general | solution.py:23
  155.5 120.2 %while.34 = (s32[]{:T(128)}, f32[128,1792]{1,0:T(8,128)S(1)}, f32[128,1792]{1,0:T(8,128)S(1)}, f32[128,1792]{1,0:T(8,128)S(1)}, f32[1792]{0:T(1024)S(1)}, /*index=5*/s32[]{:T(128)}, s32[]{:T(128)}, s32[]{:T(128)}) while((s32[]{:T(128)}, f32[128,1792]{1,0:T(8,128)S(1)}, f32[128,1792]{1,0:T(8,128)S(1)}, f32[128,1792]{1,0:T(8,128)S(1)}, ...), condition=%wide.region_1.2_spmd.clone, body=%wide.region_0.1_spmd.clone.sunk | while | flops 2293767 | bytes 8264873 | solution.py:44
  155.5 1.5 select_select_fusion.2
  157.1 2.2 collective-permute-start
  159.3 2.2 collective-permute-done
  161.5 1.5 select_select_fusion.2
  163.1 11.6 %collective-permute-start = (f32[128,1792]{1,0:T(8,128)}, f32[128,1792]{1,0:T(8,128)S(1)}, u32[]{:S(2)}, u32[]{:S(2)}) collective-permute-start(f32[128,1792]{1,0:T(8,128)} %get-tuple-element.455), channel_id=1, source_target_pairs={{0,32},{32,64},{64,96},{96,128},{128,160},{160,192},{192,224},{1,3... | collective-permute-start | bytes 2752520 | tf_op jit(solution)/shard_map/while/body/eval_jaxpr/ppermute | solution.py:12
  174.7 2.2 collective-permute-done
  176.9 1.5 select_select_fusion.2
  178.4 12.7 %collective-permute-start = (f32[128,1792]{1,0:T(8,128)}, f32[128,1792]{1,0:T(8,128)S(1)}, u32[]{:S(2)}, u32[]{:S(2)}) collective-permute-start(f32[128,1792]{1,0:T(8,128)} %get-tuple-element.455), channel_id=1, source_target_pairs={{0,32},{32,64},{64,96},{96,128},{128,160},{160,192},{192,224},{1,3... | collective-permute-start | bytes 2752520 | tf_op jit(solution)/shard_map/while/body/eval_jaxpr/ppermute | solution.py:12
  191.1 2.2 collective-permute-done
  193.3 1.5 select_select_fusion.2
  194.9 12.7 %collective-permute-start = (f32[128,1792]{1,0:T(8,128)}, f32[128,1792]{1,0:T(8,128)S(1)}, u32[]{:S(2)}, u32[]{:S(2)}) collective-permute-start(f32[128,1792]{1,0:T(8,128)} %get-tuple-element.455), channel_id=1, source_target_pairs={{0,32},{32,64},{64,96},{96,128},{128,160},{160,192},{192,224},{1,3... | collective-permute-start | bytes 2752520 | tf_op jit(solution)/shard_map/while/body/eval_jaxpr/ppermute | solution.py:12
  207.6 2.2 collective-permute-done
  209.8 1.5 select_select_fusion.2
  211.4 12.7 %collective-permute-start = (f32[128,1792]{1,0:T(8,128)}, f32[128,1792]{1,0:T(8,128)S(1)}, u32[]{:S(2)}, u32[]{:S(2)}) collective-permute-start(f32[128,1792]{1,0:T(8,128)} %get-tuple-element.455), channel_id=1, source_target_pairs={{0,32},{32,64},{64,96},{96,128},{128,160},{160,192},{192,224},{1,3... | collective-permute-start | bytes 2752520 | tf_op jit(solution)/shard_map/while/body/eval_jaxpr/ppermute | solution.py:12
  224.0 2.2 collective-permute-done
  226.3 1.5 select_select_fusion.2
  227.8 12.7 %collective-permute-start = (f32[128,1792]{1,0:T(8,128)}, f32[128,1792]{1,0:T(8,128)S(1)}, u32[]{:S(2)}, u32[]{:S(2)}) collective-permute-start(f32[128,1792]{1,0:T(8,128)} %get-tuple-element.455), channel_id=1, source_target_pairs={{0,32},{32,64},{64,96},{96,128},{128,160},{160,192},{192,224},{1,3... | collective-permute-start | bytes 2752520 | tf_op jit(solution)/shard_map/while/body/eval_jaxpr/ppermute | solution.py:12
  240.5 2.2 collective-permute-done
  242.7 1.5 select_select_fusion.2
  244.3 12.7 %collective-permute-start = (f32[128,1792]{1,0:T(8,128)}, f32[128,1792]{1,0:T(8,128)S(1)}, u32[]{:S(2)}, u32[]{:S(2)}) collective-permute-start(f32[128,1792]{1,0:T(8,128)} %get-tuple-element.455), channel_id=1, source_target_pairs={{0,32},{32,64},{64,96},{96,128},{128,160},{160,192},{192,224},{1,3... | collective-permute-start | bytes 2752520 | tf_op jit(solution)/shard_map/while/body/eval_jaxpr/ppermute | solution.py:12
  256.9 2.2 collective-permute-done
  259.2 1.5 select_select_fusion.2
  260.7 12.7 %collective-permute-start = (f32[128,1792]{1,0:T(8,128)}, f32[128,1792]{1,0:T(8,128)S(1)}, u32[]{:S(2)}, u32[]{:S(2)}) collective-permute-start(f32[128,1792]{1,0:T(8,128)} %get-tuple-element.455), channel_id=1, source_target_pairs={{0,32},{32,64},{64,96},{96,128},{128,160},{160,192},{192,224},{1,3... | collective-permute-start | bytes 2752520 | tf_op jit(solution)/shard_map/while/body/eval_jaxpr/ppermute | solution.py:12
  273.4 2.2 collective-permute-done
  275.6 1.0 copy-done
  276.7 74.4 %all-reduce.2.cloned.1.call-done = f32[128,1792]{1,0:T(8,128)} async-done(((f32[128,1792]{1,0:T(8,128)}), f32[128,1792]{1,0:T(8,128)}) %all-reduce.2.cloned.1.call-update) | async-done | bytes 917520 | tf_op jit(solution)/shard_map/psum | solution.py:47
  351.1 8.4 %fusion.4 = (f32[128,1792]{1,0:T(8,128)S(1)}, f32[128,1792]{1,0:T(8,128)S(1)}, f32[128,1792]{1,0:T(8,128)}) fusion(f32[128,1792]{1,0:T(8,128)} %copy-done, f32[128,1792]{1,0:T(8,128)} %all-reduce.2.cloned.1.call-done, f32[1792]{0:T(1024)S(1)} %get-tuple-element.528, bf16[128,3584]{1,0:T(8,128)(2,1)} %param.8, ...), kind=kOutput, calls=%fused_computation.16 | convolution fusion | flops 1646231552 | bytes 18357248 | tf_op jit(solution)/shard_map/dot_general | solution.py:24
  359.4 99.1 %while.35 = (s32[]{:T(128)}, f32[128,1792]{1,0:T(8,128)}, f32[1792]{0:T(1024)S(1)}, f32[1792]{0:T(1024)S(1)}, f32[128,1792]{1,0:T(8,128)S(1)}, /*index=5*/f32[12...) while((s32[]{:T(128)}, f32[128,1792]{1,0:T(8,128)}, ...), condition=%wide.region_5.6_spmd.clone, body=%wide.region_3.5_spmd.clone.sunk | while | flops 4132359 | bytes 7376058 | solution.py:62
  360.0 1.3 collective-permute-start.1
  361.3 2.5 collective-permute-done.1
  363.8 2.0 convert_element_type.22
  365.8 1.7 add_reduce_fusion.2
  367.5 1.3 collective-permute-start.1
  368.8 5.9 collective-permute-done.1
  374.7 2.0 convert_element_type.22
  376.8 1.7 add_reduce_fusion.2
  378.5 1.3 collective-permute-start.1
  379.8 8.6 %collective-permute-done.1 = bf16[128,1792]{1,0:T(8,128)(2,1)} collective-permute-done((bf16[128,1792]{1,0:T(8,128)(2,1)S(1)}, bf16[128,1792]{1,0:T(8,128)(2,1)}, u32[]{:S(2)}, u32[]{:S(2)}) %collective-permute-start.1) | collective-permute-done | bytes 458784 | tf_op jit(solution)/shard_map/while/body/eval_jaxpr/ppermute | solution.py:12
  388.4 2.0 convert_element_type.22
  390.4 1.7 add_reduce_fusion.2
  392.1 1.3 collective-permute-start.1
  393.4 8.6 %collective-permute-done.1 = bf16[128,1792]{1,0:T(8,128)(2,1)} collective-permute-done((bf16[128,1792]{1,0:T(8,128)(2,1)S(1)}, bf16[128,1792]{1,0:T(8,128)(2,1)}, u32[]{:S(2)}, u32[]{:S(2)}) %collective-permute-start.1) | collective-permute-done | bytes 458784 | tf_op jit(solution)/shard_map/while/body/eval_jaxpr/ppermute | solution.py:12
  402.0 2.0 convert_element_type.22
  404.0 1.7 add_reduce_fusion.2
  405.7 1.3 collective-permute-start.1
  407.0 8.6 %collective-permute-done.1 = bf16[128,1792]{1,0:T(8,128)(2,1)} collective-permute-done((bf16[128,1792]{1,0:T(8,128)(2,1)S(1)}, bf16[128,1792]{1,0:T(8,128)(2,1)}, u32[]{:S(2)}, u32[]{:S(2)}) %collective-permute-start.1) | collective-permute-done | bytes 458784 | tf_op jit(solution)/shard_map/while/body/eval_jaxpr/ppermute | solution.py:12
  415.6 2.0 convert_element_type.22
  417.6 1.7 add_reduce_fusion.2
  419.3 1.3 collective-permute-start.1
  420.7 8.6 %collective-permute-done.1 = bf16[128,1792]{1,0:T(8,128)(2,1)} collective-permute-done((bf16[128,1792]{1,0:T(8,128)(2,1)S(1)}, bf16[128,1792]{1,0:T(8,128)(2,1)}, u32[]{:S(2)}, u32[]{:S(2)}) %collective-permute-start.1) | collective-permute-done | bytes 458784 | tf_op jit(solution)/shard_map/while/body/eval_jaxpr/ppermute | solution.py:12
  429.2 2.0 convert_element_type.22
  431.3 1.7 add_reduce_fusion.2
  433.0 1.3 collective-permute-start.1
  434.3 8.6 %collective-permute-done.1 = bf16[128,1792]{1,0:T(8,128)(2,1)} collective-permute-done((bf16[128,1792]{1,0:T(8,128)(2,1)S(1)}, bf16[128,1792]{1,0:T(8,128)(2,1)}, u32[]{:S(2)}, u32[]{:S(2)}) %collective-permute-start.1) | collective-permute-done | bytes 458784 | tf_op jit(solution)/shard_map/while/body/eval_jaxpr/ppermute | solution.py:12
  442.9 2.0 convert_element_type.22
  444.9 1.7 add_reduce_fusion.2
  446.6 1.3 collective-permute-start.1
  447.9 8.6 %collective-permute-done.1 = bf16[128,1792]{1,0:T(8,128)(2,1)} collective-permute-done((bf16[128,1792]{1,0:T(8,128)(2,1)S(1)}, bf16[128,1792]{1,0:T(8,128)(2,1)}, u32[]{:S(2)}, u32[]{:S(2)}) %collective-permute-start.1) | collective-permute-done | bytes 458784 | tf_op jit(solution)/shard_map/while/body/eval_jaxpr/ppermute | solution.py:12
  456.5 2.0 convert_element_type.22
  458.5 210.8 %psum.15 = f32[1792]{0:T(1024)} all-reduce(f32[1792]{0:T(1024)S(1)} %get-tuple-element.289), channel_id=1, replica_groups=mesh['tm'=8,'mp'=4,'tok'=8] {'tm','tok'}, use_global_device_ids=true, to_apply=%region_6.7 | all-reduce | flops 1792 | bytes 14336 | tf_op jit(solution)/shard_map/psum | solution.py:65
  (21 shorter events, 0.7 us)
Async XLA Ops:
  7.2 140.9 %all-gather.2.cloned.1.call-start = ((), (), s32[]{:S(2)}) async-start(), calls=%async_computation | async-start | bytes 13045760 | tf_op jit(solution)/shard_map/all_gather | solution.py:22
  7.9 343.2 %all-reduce.2.cloned.1.call-start = ((), (), s32[]{:S(2)}) async-start(), calls=%async_computation.1 | async-start | bytes 1835008 | tf_op jit(solution)/shard_map/psum | solution.py:47
  8.0 147.5 %copy-start.2 = (f32[1792]{0:T(1024)S(1)}, f32[1792]{0:T(1024)}, u32[]{:S(2)}) copy-start(f32[1792]{0:T(1024)} %param.11) | copy-start | bytes 21508
  157.1 4.5 collective-permute-start
  163.1 13.8 %collective-permute-start = (f32[128,1792]{1,0:T(8,128)}, f32[128,1792]{1,0:T(8,128)S(1)}, u32[]{:S(2)}, u32[]{:S(2)}) collective-permute-start(f32[128,1792]{1,0:T(8,128)} %get-tuple-element.455), channel_id=1, source_target_pairs={{0,32},{32,64},{64,96},{96,128},{128,160},{160,192},{192,224},{1,3... | collective-permute-start | bytes 2752520 | tf_op jit(solution)/shard_map/while/body/eval_jaxpr/ppermute | solution.py:12
  178.4 14.9 %collective-permute-start = (f32[128,1792]{1,0:T(8,128)}, f32[128,1792]{1,0:T(8,128)S(1)}, u32[]{:S(2)}, u32[]{:S(2)}) collective-permute-start(f32[128,1792]{1,0:T(8,128)} %get-tuple-element.455), channel_id=1, source_target_pairs={{0,32},{32,64},{64,96},{96,128},{128,160},{160,192},{192,224},{1,3... | collective-permute-start | bytes 2752520 | tf_op jit(solution)/shard_map/while/body/eval_jaxpr/ppermute | solution.py:12
  194.9 14.9 %collective-permute-start = (f32[128,1792]{1,0:T(8,128)}, f32[128,1792]{1,0:T(8,128)S(1)}, u32[]{:S(2)}, u32[]{:S(2)}) collective-permute-start(f32[128,1792]{1,0:T(8,128)} %get-tuple-element.455), channel_id=1, source_target_pairs={{0,32},{32,64},{64,96},{96,128},{128,160},{160,192},{192,224},{1,3... | collective-permute-start | bytes 2752520 | tf_op jit(solution)/shard_map/while/body/eval_jaxpr/ppermute | solution.py:12
  211.4 14.9 %collective-permute-start = (f32[128,1792]{1,0:T(8,128)}, f32[128,1792]{1,0:T(8,128)S(1)}, u32[]{:S(2)}, u32[]{:S(2)}) collective-permute-start(f32[128,1792]{1,0:T(8,128)} %get-tuple-element.455), channel_id=1, source_target_pairs={{0,32},{32,64},{64,96},{96,128},{128,160},{160,192},{192,224},{1,3... | collective-permute-start | bytes 2752520 | tf_op jit(solution)/shard_map/while/body/eval_jaxpr/ppermute | solution.py:12
  227.8 14.9 %collective-permute-start = (f32[128,1792]{1,0:T(8,128)}, f32[128,1792]{1,0:T(8,128)S(1)}, u32[]{:S(2)}, u32[]{:S(2)}) collective-permute-start(f32[128,1792]{1,0:T(8,128)} %get-tuple-element.455), channel_id=1, source_target_pairs={{0,32},{32,64},{64,96},{96,128},{128,160},{160,192},{192,224},{1,3... | collective-permute-start | bytes 2752520 | tf_op jit(solution)/shard_map/while/body/eval_jaxpr/ppermute | solution.py:12
  244.3 14.9 %collective-permute-start = (f32[128,1792]{1,0:T(8,128)}, f32[128,1792]{1,0:T(8,128)S(1)}, u32[]{:S(2)}, u32[]{:S(2)}) collective-permute-start(f32[128,1792]{1,0:T(8,128)} %get-tuple-element.455), channel_id=1, source_target_pairs={{0,32},{32,64},{64,96},{96,128},{128,160},{160,192},{192,224},{1,3... | collective-permute-start | bytes 2752520 | tf_op jit(solution)/shard_map/while/body/eval_jaxpr/ppermute | solution.py:12
  260.7 14.9 %collective-permute-start = (f32[128,1792]{1,0:T(8,128)}, f32[128,1792]{1,0:T(8,128)S(1)}, u32[]{:S(2)}, u32[]{:S(2)}) collective-permute-start(f32[128,1792]{1,0:T(8,128)} %get-tuple-element.455), channel_id=1, source_target_pairs={{0,32},{32,64},{64,96},{96,128},{128,160},{160,192},{192,224},{1,3... | collective-permute-start | bytes 2752520 | tf_op jit(solution)/shard_map/while/body/eval_jaxpr/ppermute | solution.py:12
  275.6 1.0 copy-start
  276.7 82.8 %copy-start.1 = (f32[128,1792]{1,0:T(8,128)S(1)}, f32[128,1792]{1,0:T(8,128)}, u32[]{:S(2)}) copy-start(f32[128,1792]{1,0:T(8,128)} %copy-done) | copy-start | bytes 2752516
  360.0 3.8 collective-permute-start.1
  367.5 7.2 %collective-permute-start.1 = (bf16[128,1792]{1,0:T(8,128)(2,1)S(1)}, bf16[128,1792]{1,0:T(8,128)(2,1)}, u32[]{:S(2)}, u32[]{:S(2)}) collective-permute-start(bf16[128,1792]{1,0:T(8,128)(2,1)S(1)} %get-tuple-element.465), channel_id=1, source_target_pairs={{32,0},{64,32},{96,64},{128,96},{160,128},{192,160},{224,192},{33,... | collective-permute-start | bytes 1376264 | tf_op jit(solution)/shard_map/while/body/eval_jaxpr/ppermute | solution.py:12
  378.5 9.9 %collective-permute-start.1 = (bf16[128,1792]{1,0:T(8,128)(2,1)S(1)}, bf16[128,1792]{1,0:T(8,128)(2,1)}, u32[]{:S(2)}, u32[]{:S(2)}) collective-permute-start(bf16[128,1792]{1,0:T(8,128)(2,1)S(1)} %get-tuple-element.465), channel_id=1, source_target_pairs={{32,0},{64,32},{96,64},{128,96},{160,128},{192,160},{224,192},{33,... | collective-permute-start | bytes 1376264 | tf_op jit(solution)/shard_map/while/body/eval_jaxpr/ppermute | solution.py:12
  392.1 9.9 %collective-permute-start.1 = (bf16[128,1792]{1,0:T(8,128)(2,1)S(1)}, bf16[128,1792]{1,0:T(8,128)(2,1)}, u32[]{:S(2)}, u32[]{:S(2)}) collective-permute-start(bf16[128,1792]{1,0:T(8,128)(2,1)S(1)} %get-tuple-element.465), channel_id=1, source_target_pairs={{32,0},{64,32},{96,64},{128,96},{160,128},{192,160},{224,192},{33,... | collective-permute-start | bytes 1376264 | tf_op jit(solution)/shard_map/while/body/eval_jaxpr/ppermute | solution.py:12
  405.7 9.9 %collective-permute-start.1 = (bf16[128,1792]{1,0:T(8,128)(2,1)S(1)}, bf16[128,1792]{1,0:T(8,128)(2,1)}, u32[]{:S(2)}, u32[]{:S(2)}) collective-permute-start(bf16[128,1792]{1,0:T(8,128)(2,1)S(1)} %get-tuple-element.465), channel_id=1, source_target_pairs={{32,0},{64,32},{96,64},{128,96},{160,128},{192,160},{224,192},{33,... | collective-permute-start | bytes 1376264 | tf_op jit(solution)/shard_map/while/body/eval_jaxpr/ppermute | solution.py:12
  419.3 9.9 %collective-permute-start.1 = (bf16[128,1792]{1,0:T(8,128)(2,1)S(1)}, bf16[128,1792]{1,0:T(8,128)(2,1)}, u32[]{:S(2)}, u32[]{:S(2)}) collective-permute-start(bf16[128,1792]{1,0:T(8,128)(2,1)S(1)} %get-tuple-element.465), channel_id=1, source_target_pairs={{32,0},{64,32},{96,64},{128,96},{160,128},{192,160},{224,192},{33,... | collective-permute-start | bytes 1376264 | tf_op jit(solution)/shard_map/while/body/eval_jaxpr/ppermute | solution.py:12
  433.0 9.9 %collective-permute-start.1 = (bf16[128,1792]{1,0:T(8,128)(2,1)S(1)}, bf16[128,1792]{1,0:T(8,128)(2,1)}, u32[]{:S(2)}, u32[]{:S(2)}) collective-permute-start(bf16[128,1792]{1,0:T(8,128)(2,1)S(1)} %get-tuple-element.465), channel_id=1, source_target_pairs={{32,0},{64,32},{96,64},{128,96},{160,128},{192,160},{224,192},{33,... | collective-permute-start | bytes 1376264 | tf_op jit(solution)/shard_map/while/body/eval_jaxpr/ppermute | solution.py:12
  446.6 9.9 %collective-permute-start.1 = (bf16[128,1792]{1,0:T(8,128)(2,1)S(1)}, bf16[128,1792]{1,0:T(8,128)(2,1)}, u32[]{:S(2)}, u32[]{:S(2)}) collective-permute-start(bf16[128,1792]{1,0:T(8,128)(2,1)S(1)} %get-tuple-element.465), channel_id=1, source_target_pairs={{32,0},{64,32},{96,64},{128,96},{160,128},{192,160},{224,192},{33,... | collective-permute-start | bytes 1376264 | tf_op jit(solution)/shard_map/while/body/eval_jaxpr/ppermute | solution.py:12
Sparse Core Ops, SparseCore 0:
  11.7 136.3 all-gather.1
  276.8 74.2 all-reduce.1
where the time goes:
time: 677 us; the launch traced here: 676 us
  waiting for transfers between devices  293 us (43%)
  blocking collectives  211 us (31%)
  starting transfers between devices  100 us (15%)
  other arithmetic  41 us (6%)
  matrix products  15.7 us (2%)
  between operations  14.1 us (2%)
    psum x1, blocking collectives, on_device(): grad_threshold = lax.psum(grad_local, ('tm', 'tok'))  211 us
    all_gather x1, waiting for transfers between devices, on_device(): piece = lax.all_gather(gate_weight, ('tm', 'tok'), axis=0, tiled=True)  140 us
    ppermute x16, starting transfers between devices, passed_along(): return lax.ppermute(x, axis, pairs)  100 us
    ppermute x16, waiting for transfers between devices, passed_along(): return lax.ppermute(x, axis, pairs)  77.7 us
    psum x1, waiting for transfers between devices, on_device(): total = lax.psum(spikes, 'tm')  74.4 us
    convert_element_type x8, other arithmetic, backward_turn(): passed_along((incoming + dwide).astype(jnp.bfloat16), 'tm', -1)  16.3 us
  transfers between devices with their start and end apart: 18, of which 18 were waited for; matrix products, arithmetic and copies ran while one was open for 0% of the time, Pallas kernels for 0%

commit v1 on v0

--- a/solution.py
+++ b/solution.py
@@ -62,7 +62,7 @@
     unused_cot, grad_local = lax.fori_loop(
         0, turns, backward_turn, (block_zero, jnp.zeros((width,), jnp.float32))
     )
-    grad_threshold = lax.psum(grad_local, ("tm", "tok"))
+    grad_threshold = lax.psum(lax.psum(grad_local, "tm"), "tok")
     return (rates, grad_threshold)
 
 

time: 677 us -> 517 us (0.76)
  blocking collectives: 211 us -> 50.8 us
    psum x1 -> x2, blocking collectives: 211 us -> 50.8 us  [on_device(): grad_threshold = lax.psum(lax.psum(grad_local, 'tm'), 'tok')]
where the time goes in v1:
time: 517 us; the launch traced here: 516 us
  waiting for transfers between devices  293 us (57%)
  starting transfers between devices  100 us (19%)
  blocking collectives  50.8 us (10%)
  other arithmetic  40.8 us (8%)
  matrix products  15.7 us (3%)
  between operations  14.1 us (3%)
    all_gather x1, waiting for transfers between devices, on_device(): piece = lax.all_gather(gate_weight, ('tm', 'tok'), axis=0, tiled=True)  140 us
    ppermute x16, starting transfers between devices, passed_along(): return lax.ppermute(x, axis, pairs)  100 us
    ppermute x16, waiting for transfers between devices, passed_along(): return lax.ppermute(x, axis, pairs)  77.7 us
    psum x1, waiting for transfers between devices, on_device(): total = lax.psum(spikes, 'tm')  74.4 us
    psum x2, blocking collectives, on_device(): grad_threshold = lax.psum(lax.psum(grad_local, 'tm'), 'tok')  50.8 us
    convert_element_type x8, other arithmetic, backward_turn(): passed_along((incoming + dwide).astype(jnp.bfloat16), 'tm', -1)  16.1 us
    select_n x8, other arithmetic, forward_turn(): spikes = jnp.where(active, fired, older)  12.4 us
    reduce_sum x8, other arithmetic, backward_turn(): term = jnp.sum(-dwide - spikes * incoming + error * spikes / steps, axis=0)  12.3 us
  transfers between devices with their start and end apart: 18, of which 18 were waited for; matrix products, arithmetic and copies ran while one was open for 0% of the time, Pallas kernels for 0%

profile of v1, /device:TPU:32, one launch (start us, length us, event | category | flops | bytes accessed | tf_op | source)
XLA Modules:
  0.0 515.9 jit_solution(5008851999693369346)
XLA Ops:
  8.0 140.1 %all-gather.2.cloned.1.call-done = bf16[3584,1792]{1,0:T(8,128)(2,1)} async-done(((bf16[56,1792]{1,0:T(8,128)(2,1)}), bf16[3584,1792]{1,0:T(8,128)(2,1)}) %all-gather.2.cloned.1.call-update) | async-done | bytes 12845072 | tf_op jit(solution)/shard_map/all_gather | solution.py:22
  148.0 7.4 %convolution_multiply_fusion = f32[128,1792]{1,0:T(8,128)S(1)} fusion(bf16[3584,1792]{1,0:T(8,128)(2,1)} %all-gather.2.cloned.1.call-done, bf16[128,3584]{1,0:T(8,128)(2,1)} %param.8, s32[1,128,3584]{2,1,0:T(8,128)} %param.9), kind=kOutput, calls=%fused_computation.8 | convolution fusion | flops 1645314048 | bytes 16515072 | tf_op jit(solution)/shard_map/dot_general | solution.py:23
  155.5 120.2 %while.34 = (s32[]{:T(128)}, f32[128,1792]{1,0:T(8,128)S(1)}, f32[128,1792]{1,0:T(8,128)S(1)}, f32[128,1792]{1,0:T(8,128)S(1)}, f32[1792]{0:T(1024)S(1)}, /*index=5*/s32[]{:T(128)}, s32[]{:T(128)}, s32[]{:T(128)}) while((s32[]{:T(128)}, f32[128,1792]{1,0:T(8,128)S(1)}, f32[128,1792]{1,0:T(8,128)S(1)}, f32[128,1792]{1,0:T(8,128)S(1)}, ...), condition=%wide.region_1.2_spmd.clone, body=%wide.region_0.1_spmd.clone.sunk | while | flops 2293767 | bytes 8264873 | solution.py:44
  155.5 1.5 select_select_fusion.2
  157.1 2.2 collective-permute-start
  159.3 2.2 collective-permute-done
  161.5 1.5 select_select_fusion.2
  163.1 11.6 %collective-permute-start = (f32[128,1792]{1,0:T(8,128)}, f32[128,1792]{1,0:T(8,128)S(1)}, u32[]{:S(2)}, u32[]{:S(2)}) collective-permute-start(f32[128,1792]{1,0:T(8,128)} %get-tuple-element.455), channel_id=1, source_target_pairs={{0,32},{32,64},{64,96},{96,128},{128,160},{160,192},{192,224},{1,3... | collective-permute-start | bytes 2752520 | tf_op jit(solution)/shard_map/while/body/eval_jaxpr/ppermute | solution.py:12
  174.7 2.2 collective-permute-done
  176.9 1.5 select_select_fusion.2
  178.4 12.7 %collective-permute-start = (f32[128,1792]{1,0:T(8,128)}, f32[128,1792]{1,0:T(8,128)S(1)}, u32[]{:S(2)}, u32[]{:S(2)}) collective-permute-start(f32[128,1792]{1,0:T(8,128)} %get-tuple-element.455), channel_id=1, source_target_pairs={{0,32},{32,64},{64,96},{96,128},{128,160},{160,192},{192,224},{1,3... | collective-permute-start | bytes 2752520 | tf_op jit(solution)/shard_map/while/body/eval_jaxpr/ppermute | solution.py:12
  191.1 2.2 collective-permute-done
  193.3 1.5 select_select_fusion.2
  194.9 12.7 %collective-permute-start = (f32[128,1792]{1,0:T(8,128)}, f32[128,1792]{1,0:T(8,128)S(1)}, u32[]{:S(2)}, u32[]{:S(2)}) collective-permute-start(f32[128,1792]{1,0:T(8,128)} %get-tuple-element.455), channel_id=1, source_target_pairs={{0,32},{32,64},{64,96},{96,128},{128,160},{160,192},{192,224},{1,3... | collective-permute-start | bytes 2752520 | tf_op jit(solution)/shard_map/while/body/eval_jaxpr/ppermute | solution.py:12
  207.6 2.2 collective-permute-done
  209.8 1.5 select_select_fusion.2
  211.4 12.7 %collective-permute-start = (f32[128,1792]{1,0:T(8,128)}, f32[128,1792]{1,0:T(8,128)S(1)}, u32[]{:S(2)}, u32[]{:S(2)}) collective-permute-start(f32[128,1792]{1,0:T(8,128)} %get-tuple-element.455), channel_id=1, source_target_pairs={{0,32},{32,64},{64,96},{96,128},{128,160},{160,192},{192,224},{1,3... | collective-permute-start | bytes 2752520 | tf_op jit(solution)/shard_map/while/body/eval_jaxpr/ppermute | solution.py:12
  224.0 2.2 collective-permute-done
  226.3 1.5 select_select_fusion.2
  227.8 12.7 %collective-permute-start = (f32[128,1792]{1,0:T(8,128)}, f32[128,1792]{1,0:T(8,128)S(1)}, u32[]{:S(2)}, u32[]{:S(2)}) collective-permute-start(f32[128,1792]{1,0:T(8,128)} %get-tuple-element.455), channel_id=1, source_target_pairs={{0,32},{32,64},{64,96},{96,128},{128,160},{160,192},{192,224},{1,3... | collective-permute-start | bytes 2752520 | tf_op jit(solution)/shard_map/while/body/eval_jaxpr/ppermute | solution.py:12
  240.5 2.2 collective-permute-done
  242.7 1.5 select_select_fusion.2
  244.3 12.7 %collective-permute-start = (f32[128,1792]{1,0:T(8,128)}, f32[128,1792]{1,0:T(8,128)S(1)}, u32[]{:S(2)}, u32[]{:S(2)}) collective-permute-start(f32[128,1792]{1,0:T(8,128)} %get-tuple-element.455), channel_id=1, source_target_pairs={{0,32},{32,64},{64,96},{96,128},{128,160},{160,192},{192,224},{1,3... | collective-permute-start | bytes 2752520 | tf_op jit(solution)/shard_map/while/body/eval_jaxpr/ppermute | solution.py:12
  256.9 2.2 collective-permute-done
  259.2 1.5 select_select_fusion.2
  260.7 12.7 %collective-permute-start = (f32[128,1792]{1,0:T(8,128)}, f32[128,1792]{1,0:T(8,128)S(1)}, u32[]{:S(2)}, u32[]{:S(2)}) collective-permute-start(f32[128,1792]{1,0:T(8,128)} %get-tuple-element.455), channel_id=1, source_target_pairs={{0,32},{32,64},{64,96},{96,128},{128,160},{160,192},{192,224},{1,3... | collective-permute-start | bytes 2752520 | tf_op jit(solution)/shard_map/while/body/eval_jaxpr/ppermute | solution.py:12
  273.4 2.2 collective-permute-done
  275.6 1.0 copy-done
  276.7 74.4 %all-reduce.2.cloned.1.call-done = f32[128,1792]{1,0:T(8,128)} async-done(((f32[128,1792]{1,0:T(8,128)}), f32[128,1792]{1,0:T(8,128)}) %all-reduce.2.cloned.1.call-update) | async-done | bytes 917520 | tf_op jit(solution)/shard_map/psum | solution.py:47
  351.1 8.4 %fusion.4 = (f32[128,1792]{1,0:T(8,128)S(1)}, f32[128,1792]{1,0:T(8,128)S(1)}, f32[128,1792]{1,0:T(8,128)}) fusion(f32[128,1792]{1,0:T(8,128)} %copy-done, f32[128,1792]{1,0:T(8,128)} %all-reduce.2.cloned.1.call-done, f32[1792]{0:T(1024)S(1)} %get-tuple-element.528, bf16[128,3584]{1,0:T(8,128)(2,1)} %param.8, ...), kind=kOutput, calls=%fused_computation.16 | convolution fusion | flops 1646231552 | bytes 18357248 | tf_op jit(solution)/shard_map/dot_general | solution.py:24
  359.5 98.9 %while.35 = (s32[]{:T(128)}, f32[128,1792]{1,0:T(8,128)}, f32[1792]{0:T(1024)S(1)}, f32[1792]{0:T(1024)S(1)}, f32[128,1792]{1,0:T(8,128)S(1)}, /*index=5*/f32[12...) while((s32[]{:T(128)}, f32[128,1792]{1,0:T(8,128)}, ...), condition=%wide.region_5.6_spmd.clone, body=%wide.region_3.5_spmd.clone.sunk | while | flops 4132359 | bytes 7376058 | solution.py:62
  360.0 1.3 collective-permute-start.1
  361.3 2.5 collective-permute-done.1
  363.8 2.0 convert_element_type.22
  365.8 1.7 add_reduce_fusion.2
  367.5 1.3 collective-permute-start.1
  368.8 5.9 %collective-permute-done.1 = bf16[128,1792]{1,0:T(8,128)(2,1)} collective-permute-done((bf16[128,1792]{1,0:T(8,128)(2,1)S(1)}, bf16[128,1792]{1,0:T(8,128)(2,1)}, u32[]{:S(2)}, u32[]{:S(2)}) %collective-permute-start.1) | collective-permute-done | bytes 458784 | tf_op jit(solution)/shard_map/while/body/eval_jaxpr/ppermute | solution.py:12
  374.7 2.0 convert_element_type.22
  376.7 1.7 add_reduce_fusion.2
  378.4 1.3 collective-permute-start.1
  379.8 8.6 %collective-permute-done.1 = bf16[128,1792]{1,0:T(8,128)(2,1)} collective-permute-done((bf16[128,1792]{1,0:T(8,128)(2,1)S(1)}, bf16[128,1792]{1,0:T(8,128)(2,1)}, u32[]{:S(2)}, u32[]{:S(2)}) %collective-permute-start.1) | collective-permute-done | bytes 458784 | tf_op jit(solution)/shard_map/while/body/eval_jaxpr/ppermute | solution.py:12
  388.3 2.0 convert_element_type.22
  390.3 1.7 add_reduce_fusion.2
  392.0 1.3 collective-permute-start.1
  393.4 8.6 %collective-permute-done.1 = bf16[128,1792]{1,0:T(8,128)(2,1)} collective-permute-done((bf16[128,1792]{1,0:T(8,128)(2,1)S(1)}, bf16[128,1792]{1,0:T(8,128)(2,1)}, u32[]{:S(2)}, u32[]{:S(2)}) %collective-permute-start.1) | collective-permute-done | bytes 458784 | tf_op jit(solution)/shard_map/while/body/eval_jaxpr/ppermute | solution.py:12
  401.9 2.0 convert_element_type.22
  403.9 1.7 add_reduce_fusion.2
  405.6 1.3 collective-permute-start.1
  407.0 8.6 %collective-permute-done.1 = bf16[128,1792]{1,0:T(8,128)(2,1)} collective-permute-done((bf16[128,1792]{1,0:T(8,128)(2,1)S(1)}, bf16[128,1792]{1,0:T(8,128)(2,1)}, u32[]{:S(2)}, u32[]{:S(2)}) %collective-permute-start.1) | collective-permute-done | bytes 458784 | tf_op jit(solution)/shard_map/while/body/eval_jaxpr/ppermute | solution.py:12
  415.5 2.0 convert_element_type.22
  417.5 1.7 add_reduce_fusion.2
  419.2 1.3 collective-permute-start.1
  420.6 8.6 %collective-permute-done.1 = bf16[128,1792]{1,0:T(8,128)(2,1)} collective-permute-done((bf16[128,1792]{1,0:T(8,128)(2,1)S(1)}, bf16[128,1792]{1,0:T(8,128)(2,1)}, u32[]{:S(2)}, u32[]{:S(2)}) %collective-permute-start.1) | collective-permute-done | bytes 458784 | tf_op jit(solution)/shard_map/while/body/eval_jaxpr/ppermute | solution.py:12
  429.1 2.0 convert_element_type.22
  431.1 1.7 add_reduce_fusion.2
  432.8 1.3 collective-permute-start.1
  434.2 8.6 %collective-permute-done.1 = bf16[128,1792]{1,0:T(8,128)(2,1)} collective-permute-done((bf16[128,1792]{1,0:T(8,128)(2,1)S(1)}, bf16[128,1792]{1,0:T(8,128)(2,1)}, u32[]{:S(2)}, u32[]{:S(2)}) %collective-permute-start.1) | collective-permute-done | bytes 458784 | tf_op jit(solution)/shard_map/while/body/eval_jaxpr/ppermute | solution.py:12
  442.7 2.0 convert_element_type.22
  444.7 1.7 add_reduce_fusion.2
  446.4 1.3 collective-permute-start.1
  447.8 8.6 %collective-permute-done.1 = bf16[128,1792]{1,0:T(8,128)(2,1)} collective-permute-done((bf16[128,1792]{1,0:T(8,128)(2,1)S(1)}, bf16[128,1792]{1,0:T(8,128)(2,1)}, u32[]{:S(2)}, u32[]{:S(2)}) %collective-permute-start.1) | collective-permute-done | bytes 458784 | tf_op jit(solution)/shard_map/while/body/eval_jaxpr/ppermute | solution.py:12
  456.3 2.0 convert_element_type.22
  458.3 19.2 %psum.22 = f32[1792]{0:T(1024)S(1)} all-reduce(f32[1792]{0:T(1024)S(1)} %get-tuple-element.289), channel_id=1, replica_groups=mesh['tm'=8,'mp'=4,'tok'=8] {'tm'}, use_global_device_ids=true, to_apply=%region_6.7 | all-reduce | flops 1792 | bytes 14336 | tf_op jit(solution)/shard_map/psum | solution.py:65
  477.5 31.6 %psum.23 = f32[1792]{0:T(1024)} all-reduce(f32[1792]{0:T(1024)S(1)} %psum.22), channel_id=1, replica_groups=mesh['tm'=8,'mp'=4,'tok'=8] {'tok'}, use_global_device_ids=true, to_apply=%region_7.8 | all-reduce | flops 1792 | bytes 14336 | tf_op jit(solution)/shard_map/psum | solution.py:65
  (22 shorter events, 1.4 us)
Async XLA Ops:
  7.2 140.9 %all-gather.2.cloned.1.call-start = ((), (), s32[]{:S(2)}) async-start(), calls=%async_computation | async-start | bytes 13045760 | tf_op jit(solution)/shard_map/all_gather | solution.py:22
  7.9 343.2 %all-reduce.2.cloned.1.call-start = ((), (), s32[]{:S(2)}) async-start(), calls=%async_computation.1 | async-start | bytes 1835008 | tf_op jit(solution)/shard_map/psum | solution.py:47
  8.0 147.5 %copy-start.2 = (f32[1792]{0:T(1024)S(1)}, f32[1792]{0:T(1024)}, u32[]{:S(2)}) copy-start(f32[1792]{0:T(1024)} %param.11) | copy-start | bytes 21508
  157.1 4.5 collective-permute-start
  163.1 13.8 %collective-permute-start = (f32[128,1792]{1,0:T(8,128)}, f32[128,1792]{1,0:T(8,128)S(1)}, u32[]{:S(2)}, u32[]{:S(2)}) collective-permute-start(f32[128,1792]{1,0:T(8,128)} %get-tuple-element.455), channel_id=1, source_target_pairs={{0,32},{32,64},{64,96},{96,128},{128,160},{160,192},{192,224},{1,3... | collective-permute-start | bytes 2752520 | tf_op jit(solution)/shard_map/while/body/eval_jaxpr/ppermute | solution.py:12
  178.4 14.9 %collective-permute-start = (f32[128,1792]{1,0:T(8,128)}, f32[128,1792]{1,0:T(8,128)S(1)}, u32[]{:S(2)}, u32[]{:S(2)}) collective-permute-start(f32[128,1792]{1,0:T(8,128)} %get-tuple-element.455), channel_id=1, source_target_pairs={{0,32},{32,64},{64,96},{96,128},{128,160},{160,192},{192,224},{1,3... | collective-permute-start | bytes 2752520 | tf_op jit(solution)/shard_map/while/body/eval_jaxpr/ppermute | solution.py:12
  194.9 14.9 %collective-permute-start = (f32[128,1792]{1,0:T(8,128)}, f32[128,1792]{1,0:T(8,128)S(1)}, u32[]{:S(2)}, u32[]{:S(2)}) collective-permute-start(f32[128,1792]{1,0:T(8,128)} %get-tuple-element.455), channel_id=1, source_target_pairs={{0,32},{32,64},{64,96},{96,128},{128,160},{160,192},{192,224},{1,3... | collective-permute-start | bytes 2752520 | tf_op jit(solution)/shard_map/while/body/eval_jaxpr/ppermute | solution.py:12
  211.4 14.9 %collective-permute-start = (f32[128,1792]{1,0:T(8,128)}, f32[128,1792]{1,0:T(8,128)S(1)}, u32[]{:S(2)}, u32[]{:S(2)}) collective-permute-start(f32[128,1792]{1,0:T(8,128)} %get-tuple-element.455), channel_id=1, source_target_pairs={{0,32},{32,64},{64,96},{96,128},{128,160},{160,192},{192,224},{1,3... | collective-permute-start | bytes 2752520 | tf_op jit(solution)/shard_map/while/body/eval_jaxpr/ppermute | solution.py:12
  227.8 14.9 %collective-permute-start = (f32[128,1792]{1,0:T(8,128)}, f32[128,1792]{1,0:T(8,128)S(1)}, u32[]{:S(2)}, u32[]{:S(2)}) collective-permute-start(f32[128,1792]{1,0:T(8,128)} %get-tuple-element.455), channel_id=1, source_target_pairs={{0,32},{32,64},{64,96},{96,128},{128,160},{160,192},{192,224},{1,3... | collective-permute-start | bytes 2752520 | tf_op jit(solution)/shard_map/while/body/eval_jaxpr/ppermute | solution.py:12
  244.3 14.9 %collective-permute-start = (f32[128,1792]{1,0:T(8,128)}, f32[128,1792]{1,0:T(8,128)S(1)}, u32[]{:S(2)}, u32[]{:S(2)}) collective-permute-start(f32[128,1792]{1,0:T(8,128)} %get-tuple-element.455), channel_id=1, source_target_pairs={{0,32},{32,64},{64,96},{96,128},{128,160},{160,192},{192,224},{1,3... | collective-permute-start | bytes 2752520 | tf_op jit(solution)/shard_map/while/body/eval_jaxpr/ppermute | solution.py:12
  260.7 14.9 %collective-permute-start = (f32[128,1792]{1,0:T(8,128)}, f32[128,1792]{1,0:T(8,128)S(1)}, u32[]{:S(2)}, u32[]{:S(2)}) collective-permute-start(f32[128,1792]{1,0:T(8,128)} %get-tuple-element.455), channel_id=1, source_target_pairs={{0,32},{32,64},{64,96},{96,128},{128,160},{160,192},{192,224},{1,3... | collective-permute-start | bytes 2752520 | tf_op jit(solution)/shard_map/while/body/eval_jaxpr/ppermute | solution.py:12
  275.6 1.0 copy-start
  276.7 82.8 %copy-start.1 = (f32[128,1792]{1,0:T(8,128)S(1)}, f32[128,1792]{1,0:T(8,128)}, u32[]{:S(2)}) copy-start(f32[128,1792]{1,0:T(8,128)} %copy-done) | copy-start | bytes 2752516
  360.0 3.8 collective-permute-start.1
  367.5 7.2 %collective-permute-start.1 = (bf16[128,1792]{1,0:T(8,128)(2,1)S(1)}, bf16[128,1792]{1,0:T(8,128)(2,1)}, u32[]{:S(2)}, u32[]{:S(2)}) collective-permute-start(bf16[128,1792]{1,0:T(8,128)(2,1)S(1)} %get-tuple-element.465), channel_id=1, source_target_pairs={{32,0},{64,32},{96,64},{128,96},{160,128},{192,160},{224,192},{33,... | collective-permute-start | bytes 1376264 | tf_op jit(solution)/shard_map/while/body/eval_jaxpr/ppermute | solution.py:12
  378.4 9.9 %collective-permute-start.1 = (bf16[128,1792]{1,0:T(8,128)(2,1)S(1)}, bf16[128,1792]{1,0:T(8,128)(2,1)}, u32[]{:S(2)}, u32[]{:S(2)}) collective-permute-start(bf16[128,1792]{1,0:T(8,128)(2,1)S(1)} %get-tuple-element.465), channel_id=1, source_target_pairs={{32,0},{64,32},{96,64},{128,96},{160,128},{192,160},{224,192},{33,... | collective-permute-start | bytes 1376264 | tf_op jit(solution)/shard_map/while/body/eval_jaxpr/ppermute | solution.py:12
  392.0 9.9 %collective-permute-start.1 = (bf16[128,1792]{1,0:T(8,128)(2,1)S(1)}, bf16[128,1792]{1,0:T(8,128)(2,1)}, u32[]{:S(2)}, u32[]{:S(2)}) collective-permute-start(bf16[128,1792]{1,0:T(8,128)(2,1)S(1)} %get-tuple-element.465), channel_id=1, source_target_pairs={{32,0},{64,32},{96,64},{128,96},{160,128},{192,160},{224,192},{33,... | collective-permute-start | bytes 1376264 | tf_op jit(solution)/shard_map/while/body/eval_jaxpr/ppermute | solution.py:12
  405.6 9.9 %collective-permute-start.1 = (bf16[128,1792]{1,0:T(8,128)(2,1)S(1)}, bf16[128,1792]{1,0:T(8,128)(2,1)}, u32[]{:S(2)}, u32[]{:S(2)}) collective-permute-start(bf16[128,1792]{1,0:T(8,128)(2,1)S(1)} %get-tuple-element.465), channel_id=1, source_target_pairs={{32,0},{64,32},{96,64},{128,96},{160,128},{192,160},{224,192},{33,... | collective-permute-start | bytes 1376264 | tf_op jit(solution)/shard_map/while/body/eval_jaxpr/ppermute | solution.py:12
  419.2 9.9 %collective-permute-start.1 = (bf16[128,1792]{1,0:T(8,128)(2,1)S(1)}, bf16[128,1792]{1,0:T(8,128)(2,1)}, u32[]{:S(2)}, u32[]{:S(2)}) collective-permute-start(bf16[128,1792]{1,0:T(8,128)(2,1)S(1)} %get-tuple-element.465), channel_id=1, source_target_pairs={{32,0},{64,32},{96,64},{128,96},{160,128},{192,160},{224,192},{33,... | collective-permute-start | bytes 1376264 | tf_op jit(solution)/shard_map/while/body/eval_jaxpr/ppermute | solution.py:12
  432.8 9.9 %collective-permute-start.1 = (bf16[128,1792]{1,0:T(8,128)(2,1)S(1)}, bf16[128,1792]{1,0:T(8,128)(2,1)}, u32[]{:S(2)}, u32[]{:S(2)}) collective-permute-start(bf16[128,1792]{1,0:T(8,128)(2,1)S(1)} %get-tuple-element.465), channel_id=1, source_target_pairs={{32,0},{64,32},{96,64},{128,96},{160,128},{192,160},{224,192},{33,... | collective-permute-start | bytes 1376264 | tf_op jit(solution)/shard_map/while/body/eval_jaxpr/ppermute | solution.py:12
  446.4 9.9 %collective-permute-start.1 = (bf16[128,1792]{1,0:T(8,128)(2,1)S(1)}, bf16[128,1792]{1,0:T(8,128)(2,1)}, u32[]{:S(2)}, u32[]{:S(2)}) collective-permute-start(bf16[128,1792]{1,0:T(8,128)(2,1)S(1)} %get-tuple-element.465), channel_id=1, source_target_pairs={{32,0},{64,32},{96,64},{128,96},{160,128},{192,160},{224,192},{33,... | collective-permute-start | bytes 1376264 | tf_op jit(solution)/shard_map/while/body/eval_jaxpr/ppermute | solution.py:12
Sparse Core Ops, SparseCore 0:
  11.7 136.3 all-gather.1
  276.8 74.2 all-reduce.1
